TPU v7x, 32 devices: a whole 2x2x4 slice. The times are simulated.
32 devices in a mesh: parts: 2 (over x), grid: 8 (over z, y), depth: 2 (over core).
Axes of the slice: x: 2, y: 2, z: 4, core: 2. Of those that a mesh axis runs over, the one named last changes fastest.
Arguments:
- gate_input: bfloat16 [1024, 32768], P(('parts', 'depth'), 'grid'), parts along dimension 0, may hold values from -6 to 6
- up_input: bfloat16 [1024, 32768], P(('parts', 'depth'), 'grid'), parts along dimension 0, may hold values from -6 to 6
- code_values: bfloat16 [32768, 8192], P('grid', 'depth'), may hold values from -6 to 6, as said below
- exponents: int32 [1024, 8192], P('grid', 'depth'), may hold values from -10 to -7
- cotangent: bfloat16 [1024, 8192], P(('parts', 'depth'), 'grid'), parts along dimension 0, may hold values from -1.5 to 1.5
Outputs:
- output_rows: bfloat16 [1024, 8192], P(('parts', 'depth'), 'grid'), parts along dimension 0
- grad_gate: bfloat16 [1024, 32768], P(('parts', 'depth'), 'grid'), parts along dimension 0
- grad_up: bfloat16 [1024, 32768], P(('parts', 'depth'), 'grid'), parts along dimension 0
- grad_weight: bfloat16 [65536, 8192], P(('parts', 'grid'), 'depth'), parts along dimension 0
There are 2 independent parts, one for each index of `parts`. A program takes and returns all parts, laid end to end along the dimension named above; an argument that names none is the same for every part. Nothing has to cross between parts.
Inputs may be any that keep to these rules, and one draw needn't show every extreme that they name: `code_values`: every entry is one of the E2M1 values 0, +-0.5, +-1, +-1.5, +-2, +-3, +-4, +-6.
All inputs are finite; a program needn't handle non-finite values.
Results may differ from a plain program's by a relative error of at most 0.0049.
Values may be sent and summed in bfloat16 or wider, within the bound.
No kernel may reach another device: no remote copies, remote signals or barrier semaphores. Data moves between devices by JAX's collectives and lax.ppermute only.
A program may use at most 448 MiB of HBM per device.

v0:
```python
import jax
import jax.numpy as jnp
from jax import lax
from jax.sharding import PartitionSpec as P


def shards(gate_input, up_input, code_values, exponents, cotangent):
    local_units = code_values.shape[0]
    scaled = jnp.exp2(exponents.astype(jnp.float32))
    blocks = code_values.astype(jnp.float32).reshape(local_units // 32, 32, -1) * scaled[:, None, :]
    weight_part = blocks.reshape(local_units, -1).astype(jnp.bfloat16)
    weight = lax.all_gather(weight_part, "depth", axis=1, tiled=True)
    gate_float = gate_input.astype(jnp.float32)
    up_float = up_input.astype(jnp.float32)
    sigmoid_gate = jax.nn.sigmoid(gate_float)
    activated = gate_float * sigmoid_gate
    hidden = (activated * up_float).astype(jnp.bfloat16)
    summed = lax.psum_scatter(
        lax.dot_general(
            weight, hidden, (((0,), (1,)), ((), ())), preferred_element_type=jnp.float32
        ),
        "grid",
        scatter_dimension=0,
        tiled=True,
    )
    output_rows = summed.T.astype(jnp.bfloat16)
    cotangent_all = lax.all_gather(cotangent, "grid", axis=1, tiled=True)
    grad_hidden = lax.dot_general(
        cotangent_all, weight, (((1,), (1,)), ((), ())), preferred_element_type=jnp.float32
    )
    slope = sigmoid_gate * (1.0 + gate_float * (1.0 - sigmoid_gate))
    grad_gate = (grad_hidden * up_float * slope).astype(jnp.bfloat16)
    grad_up = (grad_hidden * activated).astype(jnp.bfloat16)
    weight_term = lax.dot_general(
        hidden, cotangent_all, (((0,), (0,)), ((), ())), preferred_element_type=jnp.float32
    )
    grad_weight = lax.psum_scatter(weight_term, "depth", scatter_dimension=1, tiled=True).astype(
        jnp.bfloat16
    )
    return (output_rows, grad_gate, grad_up, grad_weight)


def solution(mesh):
    in_specs = (
        P(("parts", "depth"), "grid"),
        P(("parts", "depth"), "grid"),
        P("grid", "depth"),
        P("grid", "depth"),
        P(("parts", "depth"), "grid"),
    )
    out_specs = (
        P(("parts", "depth"), "grid"),
        P(("parts", "depth"), "grid"),
        P(("parts", "depth"), "grid"),
        P(("parts", "grid"), "depth"),
    )
    return jax.shard_map(shards, mesh=mesh, in_specs=in_specs, out_specs=out_specs, check_vma=False)
```

profile of v0, /device:TPU:0, one launch (start us, length us, event | category | flops | bytes accessed | tf_op | source)
XLA Modules:
  0.0 557.2 jit_solution(14383094031951518844)
XLA Ops:
  7.2 0.0 all-gather.3.cloned.1.call-start
  7.2 1.9 multiply_exponential_fusion
  9.1 23.3 %fusion = bf16[4096,4096]{1,0:T(8,128)(2,1)} fusion(bf16[4096,4096]{1,0:T(8,128)(2,1)} %param.7, f32[128,4096]{1,0:T(8,128)S(1)} %multiply_exponential_fusion), kind=kLoop, calls=%fused_computation.1 | loop fusion | flops 50331648 | bytes 69206016 | tf_op jit(solution)/shard_map/convert_element_type | solution.py:11
  32.3 0.0 all-gather.3.cloned.1.call-update
  32.4 0.0 all-gather.5.cloned.1.call-start
  32.4 0.7 all-gather.5.cloned.1.call-update
  33.1 0.0 reduce-scatter.3.cloned.1.call-start
  33.2 3.3 copy.9
  36.5 4.1 copy.10
  40.5 89.8 %all-gather.3.cloned.1.call-done = bf16[4096,8192]{1,0:T(8,128)(2,1)} async-done(((bf16[4096,4096]{1,0:T(8,128)(2,1)}), bf16[4096,8192]{1,0:T(8,128)(2,1)}) %all-gather.3.cloned.1.call-update) | async-done | bytes 67108880 | tf_op jit(solution)/shard_map/all_gather | solution.py:12
  130.3 30.2 %fusion.11 = f32[8192,256]{1,0:T(8,128)} fusion(bf16[4096,8192]{1,0:T(8,128)(2,1)} %all-gather.3.cloned.1.call-done, bf16[256,4096]{0,1:T(8,128)(2,1)} %copy.10, bf16[256,4096]{0,1:T(8,128)(2,1)S(1)} %copy.9), kind=kOutput, calls=%fused_computation.20 | convolution fusion | flops 17188257792 | bytes 79691776 | tf_op jit(solution)/shard_map/dot_general | solution.py:19
  160.5 0.0 reduce-scatter.3.cloned.1.call-update
  160.5 0.2 reduce-scatter.5.cloned.1.call-start
  160.8 46.3 %all-gather.5.cloned.1.call-done = bf16[256,8192]{1,0:T(8,128)(2,1)} async-done(((bf16[256,1024]{1,0:T(8,128)(2,1)}), bf16[256,8192]{1,0:T(8,128)(2,1)}) %all-gather.5.cloned.1.call-update) | async-done | bytes 4194320 | tf_op jit(solution)/shard_map/all_gather | solution.py:27
  207.1 49.9 %fusion.9 = f32[4096,8192]{1,0:T(8,128)} fusion(bf16[256,8192]{1,0:T(8,128)(2,1)} %all-gather.5.cloned.1.call-done, bf16[256,4096]{0,1:T(8,128)(2,1)} %copy.10, bf16[256,4096]{0,1:T(8,128)(2,1)S(1)} %copy.9), kind=kOutput, calls=%fused_computation.19 | convolution fusion | flops 17188257792 | bytes 142606336 | tf_op jit(solution)/shard_map/dot_general | solution.py:34
  257.0 0.0 reduce-scatter.5.cloned.1.call-update
  257.1 29.7 %multiply_convert_fusion = (bf16[256,4096]{0,1:T(8,128)(2,1)}, bf16[256,4096]{0,1:T(8,128)(2,1)}) fusion(bf16[256,4096]{0,1:T(8,128)(2,1)S(1)} %copy.9, bf16[256,4096]{0,1:T(8,128)(2,1)} %copy.10, bf16[4096,8192]{1,0:T(8,128)(2,1)} %all-gather.3.cloned.1.call-done, bf16[256,8192]{1,0:T(8,128)(2,1)} %all-gather.5.cloned.1.call-done), kind=kOutput, calls=%fused_computation.16 | convolution fusion | flops 17195597824 | bytes 79691776 | tf_op jit(solution)/shard_map/dot_general | solution.py:28
  286.7 0.0 copy-start
  286.7 4.3 copy.13
  291.0 0.0 copy-done
  291.0 2.8 copy.12
  293.9 64.7 %reduce-scatter.3.cloned.1.call-done = f32[1024,256]{1,0:T(8,128)} async-done(((f32[8192,256]{1,0:T(8,128)}), f32[1024,256]{1,0:T(8,128)}) %reduce-scatter.3.cloned.1.call-update) | async-done | bytes 1048592 | tf_op jit(solution)/shard_map/reduce_scatter | solution.py:18
  358.6 1.3 convert_bitcast_fusion
  359.8 1.0 copy.11
  360.8 157.4 %reduce-scatter.5.cloned.1.call-done = f32[4096,4096]{1,0:T(8,128)} async-done(((f32[4096,8192]{1,0:T(8,128)}), f32[4096,4096]{1,0:T(8,128)}) %reduce-scatter.5.cloned.1.call-update) | async-done | bytes 67108880 | tf_op jit(solution)/shard_map/reduce_scatter | solution.py:37
  518.3 32.4 %convert_element_type.43 = bf16[4096,4096]{1,0:T(8,128)(2,1)} convert(f32[4096,4096]{1,0:T(8,128)} %reduce-scatter.5.cloned.1.call-done) | non-fusion elementwise | flops 16777216 | bytes 100663296 | tf_op jit(solution)/shard_map/convert_element_type | solution.py:37
Async XLA Ops:
  7.2 123.2 %all-gather.3.cloned.1.call-start = ((), (), s32[]{:S(2)}) async-start(), calls=%async_computation.2 | async-start | bytes 100663296 | tf_op jit(solution)/shard_map/all_gather | solution.py:12
  32.4 174.7 %all-gather.5.cloned.1.call-start = ((), (), s32[]{:S(2)}) async-start(), calls=%async_computation.4 | async-start | bytes 4718592 | tf_op jit(solution)/shard_map/all_gather | solution.py:27
  33.1 325.4 %reduce-scatter.3.cloned.1.call-start = ((), (), s32[]{:S(2)}) async-start(), calls=%async_computation.3 | async-start | bytes 9437184 | tf_op jit(solution)/shard_map/reduce_scatter | solution.py:18
  160.5 357.7 %reduce-scatter.5.cloned.1.call-start = ((), (), s32[]{:S(2)}) async-start(), calls=%async_computation.5 | async-start | bytes 201326592 | tf_op jit(solution)/shard_map/reduce_scatter | solution.py:37
  286.7 4.3 copy-start
Sparse Core Ops, SparseCore 0:
  32.5 97.7 all-gather.2
  132.5 74.5 all-gather.4
  211.3 147.2 reduce-scatter.2
  360.8 157.4 reduce-scatter.4
where the time goes:
time: 558 us; the launch traced here: 557 us
  waiting for transfers between devices  359 us (64%)
  matrix products  110 us (20%)
  other arithmetic  58.8 us (11%)
  local copies, waits for them, and re-layouts  15.5 us (3%)
  between operations  13.8 us (2%)
    reduce_scatter x1, waiting for transfers between devices, shards(): lax.psum_scatter(weight_term, 'depth', scatter_dimension=1, tiled=True)  157 us
    all_gather x1, waiting for transfers between devices, shards(): weight = lax.all_gather(weight_part, 'depth', axis=1, tiled=True)  89.8 us
    reduce_scatter x1, waiting for transfers between devices, shards(): lax.psum_scatter(lax.dot_general(weight, hidden, (((0,), (1,)), ((), ()))...  64.7 us
    dot_general x1, matrix products, shards(): lax.dot_general(hidden, cotangent_all, (((0,), (0,)), ((), ())), preferre...  49.9 us
    all_gather x1, waiting for transfers between devices, shards(): cotangent_all = lax.all_gather(cotangent, 'grid', axis=1, tiled=True)  46.3 us
    convert_element_type x1, other arithmetic, shards(): lax.psum_scatter(weight_term, 'depth', scatter_dimension=1, tiled=True)  32.4 us
    dot_general x1, matrix products, shards(): lax.dot_general(weight, hidden, (((0,), (1,)), ((), ())), preferred_eleme...  30.2 us
    dot_general x1, matrix products, shards(): lax.dot_general(cotangent_all, weight, (((1,), (1,)), ((), ())), preferre...  29.7 us
  transfers between devices with their start and end apart: 4, of which 4 were waited for; matrix products, arithmetic and copies ran while one was open for 23% of the time, Pallas kernels for 0%

commit v1 on v0

v1 whole, which is shorter than its diff:
```python
import jax
import jax.numpy as jnp
from jax import lax
from jax.experimental import pallas as pl
from jax.experimental.pallas import tpu as pltpu
from jax.sharding import PartitionSpec as P

F32 = jnp.float32
BF16 = jnp.bfloat16
VMEM_BYTES = 56 * 1024 * 1024


def tile_of(size, wanted):
    return min(size, wanted)


def dequantize(codes, scale):
    rows, columns = codes.shape
    blocks = codes.reshape(rows // 32, 32, columns) * scale.reshape(rows // 32, 1, columns)
    return blocks.reshape(rows, columns)


def output_term(hidden, codes, scale):
    tokens, units = hidden.shape
    features = codes.shape[1]
    tile = tile_of(features, 512)
    step = tile_of(units, 1024)

    def body(h_ref, c_ref, s_ref, o_ref):
        total = jnp.zeros((tokens, tile), F32)
        for k in range(0, units, step):
            weight = dequantize(c_ref[k : k + step, :], s_ref[k // 32 : (k + step) // 32, :])
            total += jnp.dot(h_ref[:, k : k + step], weight, preferred_element_type=F32)
        o_ref[...] = total.astype(BF16)

    return pl.pallas_call(
        body,
        grid=(features // tile,),
        in_specs=[
            pl.BlockSpec((tokens, units), lambda j: (0, 0)),
            pl.BlockSpec((units, tile), lambda j: (0, j)),
            pl.BlockSpec((units // 32, tile), lambda j: (0, j)),
        ],
        out_specs=pl.BlockSpec((tokens, tile), lambda j: (0, j)),
        out_shape=jax.ShapeDtypeStruct((tokens, features), BF16),
        compiler_params=pltpu.CompilerParams(vmem_limit_bytes=VMEM_BYTES),
        cost_estimate=pl.CostEstimate(
            flops=2 * tokens * units * features, bytes_accessed=2 * units * features, transcendentals=0
        ),
    )(hidden, codes, scale)


def hidden_gradient(cotangent, codes, scale):
    tokens, features = cotangent.shape
    units = codes.shape[0]
    tile = tile_of(units, 512)
    step = tile_of(features, 1024)

    def body(t_ref, c_ref, s_ref, o_ref):
        total = jnp.zeros((tokens, tile), F32)
        for k in range(0, features, step):
            weight = dequantize(c_ref[:, k : k + step], s_ref[:, k : k + step])
            total += lax.dot_general(
                t_ref[:, k : k + step], weight, (((1,), (1,)), ((), ())), preferred_element_type=F32
            )
        o_ref[...] = total

    return pl.pallas_call(
        body,
        grid=(units // tile,),
        in_specs=[
            pl.BlockSpec((tokens, features), lambda j: (0, 0)),
            pl.BlockSpec((tile, features), lambda j: (j, 0)),
            pl.BlockSpec((tile // 32, features), lambda j: (j, 0)),
        ],
        out_specs=pl.BlockSpec((tokens, tile), lambda j: (0, j)),
        out_shape=jax.ShapeDtypeStruct((tokens, units), F32),
        compiler_params=pltpu.CompilerParams(vmem_limit_bytes=VMEM_BYTES),
        cost_estimate=pl.CostEstimate(
            flops=2 * tokens * units * features, bytes_accessed=2 * units * features, transcendentals=0
        ),
    )(cotangent, codes, scale)


def weight_gradient(hidden, cotangent):
    tokens, units = hidden.shape
    features = cotangent.shape[1]
    tile = tile_of(units, 512)
    step = tile_of(features, 1024)

    def body(h_ref, t_ref, o_ref):
        turned = h_ref[...].T
        for k in range(0, features, step):
            o_ref[:, k : k + step] = jnp.dot(
                turned, t_ref[:, k : k + step], preferred_element_type=F32
            ).astype(BF16)

    return pl.pallas_call(
        body,
        grid=(units // tile,),
        in_specs=[
            pl.BlockSpec((tokens, tile), lambda j: (0, j)),
            pl.BlockSpec((tokens, features), lambda j: (0, 0)),
        ],
        out_specs=pl.BlockSpec((tile, features), lambda j: (j, 0)),
        out_shape=jax.ShapeDtypeStruct((units, features), BF16),
        compiler_params=pltpu.CompilerParams(vmem_limit_bytes=VMEM_BYTES),
        cost_estimate=pl.CostEstimate(
            flops=2 * tokens * units * features, bytes_accessed=2 * units * features, transcendentals=0
        ),
    )(hidden, cotangent)


def shards(n, gate_input, up_input, code_values, exponents, cotangent):
    tokens, part = cotangent.shape
    me = lax.axis_index("depth")
    swap = [(0, 1), (1, 0)]
    half = n // 2

    gathered = lax.all_gather(cotangent, "grid", axis=0, tiled=False)

    gate_float = gate_input.astype(F32)
    up_float = up_input.astype(F32)
    hidden = (gate_float * jax.nn.sigmoid(gate_float) * up_float).astype(BF16)
    scale = jnp.exp2(exponents.astype(F32)).astype(BF16)
    hidden_both = jnp.concatenate([hidden, lax.ppermute(hidden, "depth", swap)], 0)

    partial = output_term(hidden_both, code_values, scale)
    received = lax.ppermute(partial[tokens:], "depth", swap)
    mine = partial[:tokens]
    first = jnp.where(me == 0, mine, received).reshape(tokens, half, part)
    second = jnp.where(me == 0, received, mine).reshape(tokens, half, part)
    pieces = jnp.concatenate([first, second], 1).transpose(1, 0, 2)
    output_rows = lax.psum_scatter(pieces, "grid", scatter_dimension=0, tiled=False)

    keep = lax.dynamic_slice_in_dim(gathered, me * half, half, 0)
    give = lax.dynamic_slice_in_dim(gathered, (1 - me) * half, half, 0)
    got = lax.ppermute(give, "depth", swap)
    cotangent_both = jnp.concatenate([keep, got], 1).transpose(1, 0, 2).reshape(2 * tokens, half * part)

    partial_grad = hidden_gradient(cotangent_both, code_values, scale)
    other_grad = lax.ppermute(partial_grad[tokens:].astype(BF16), "depth", swap)
    grad_weight = weight_gradient(hidden_both, cotangent_both)

    grad_hidden = partial_grad[:tokens] + other_grad.astype(F32)
    gate_float = gate_input.astype(F32)
    up_float = up_input.astype(F32)
    sigmoid_gate = jax.nn.sigmoid(gate_float)
    slope = sigmoid_gate * (1.0 + gate_float * (1.0 - sigmoid_gate))
    grad_gate = (grad_hidden * up_float * slope).astype(BF16)
    grad_up = (grad_hidden * (gate_float * sigmoid_gate)).astype(BF16)
    return (output_rows, grad_gate, grad_up, grad_weight)


def solution(mesh):
    n = mesh.shape["grid"]
    in_specs = (
        P(("parts", "depth"), "grid"),
        P(("parts", "depth"), "grid"),
        P("grid", "depth"),
        P("grid", "depth"),
        P(("parts", "depth"), "grid"),
    )
    out_specs = (
        P(("parts", "depth"), "grid"),
        P(("parts", "depth"), "grid"),
        P(("parts", "depth"), "grid"),
        P(("parts", "grid"), "depth"),
    )

    def step(*arrays):
        return shards(n, *arrays)

    return jax.shard_map(step, mesh=mesh, in_specs=in_specs, out_specs=out_specs, check_vma=False)
```

time: 558 us -> 273 us (0.49)
  waiting for transfers between devices: 359 us -> 155 us
  matrix products: 110 us -> 0 us
  Pallas kernels: 0 us -> 71 us
  other arithmetic: 58.8 us -> 17.1 us
    reduce_scatter x2 -> x1, waiting for transfers between devices: 222 us -> 62.8 us  [shards(): lax.psum_scatter(pieces, 'grid', scatter_dimension=0, tiled=False)]
    dot_general x3 -> x0, matrix products: 110 us -> none  [the longest x1 49.9 us: shards(): lax.dot_general(hidden, cotangent_all, (((0,), (0,)), ((), ())), preferre...]
    pallas_call x0 -> x3, Pallas kernels: none -> 71 us  [the longest x1 24.2 us: hidden_gradient(): pl.pallas_call(body, grid=(units // tile,), in_specs=[pl.BlockSpec((token...]
    all_gather x2 -> x1, waiting for transfers between devices: 136 us -> 78.3 us  [shards(): gathered = lax.all_gather(cotangent, 'grid', axis=0, tiled=False)]
    convert_element_type x3 -> x2, other arithmetic: 56.9 us -> 7.1 us  [the longest x1 5.71 us: shards(): grad_up = (grad_hidden * (gate_float * sigmoid_gate)).astype(BF16)]
    ppermute x0 -> x4, waiting for transfers between devices: none -> 13.3 us  [the longest x1 4.15 us: shards(): received = lax.ppermute(partial[tokens:], 'depth', swap)]
    unnamed x7 -> x9, local copies, waits for them, and re-layouts: 15.5 us -> 7.49 us
  transfers between devices with their start and end apart: 4 -> 6, of which waited for: 4 -> 6; matrix products, arithmetic and copies ran while one was open for 23% -> 1% of each run, Pallas kernels for 0% -> 9%
where the time goes in v1:
time: 273 us
  waiting for transfers between devices  155 us (57%)
  Pallas kernels  71 us (26%)
  other arithmetic  17.1 us (6%)
  local copies, waits for them, and re-layouts  15 us (5%)
  between operations  14.1 us (5%)
    all_gather x1, waiting for transfers between devices, shards(): gathered = lax.all_gather(cotangent, 'grid', axis=0, tiled=False)  78.3 us
    reduce_scatter x1, waiting for transfers between devices, shards(): lax.psum_scatter(pieces, 'grid', scatter_dimension=0, tiled=False)  62.8 us
    pallas_call x1, Pallas kernels, hidden_gradient(): pl.pallas_call(body, grid=(units // tile,), in_specs=[pl.BlockSpec((token...  24.2 us
    pallas_call x1, Pallas kernels, weight_gradient(): pl.pallas_call(body, grid=(units // tile,), in_specs=[pl.BlockSpec((token...  23.5 us
    pallas_call x1, Pallas kernels, output_term(): pl.pallas_call(body, grid=(features // tile,), in_specs=[pl.BlockSpec((to...  23.3 us
    unnamed x9, local copies, waits for them, and re-layouts  7.49 us
    convert_element_type x1, other arithmetic, shards(): grad_up = (grad_hidden * (gate_float * sigmoid_gate)).astype(BF16)  5.71 us
  transfers between devices with their start and end apart: 6, of which 6 were waited for; matrix products, arithmetic and copies ran while one was open for 1% of the time, Pallas kernels for 9%

profile of v1, /device:TPU:0, one launch (start us, length us, event | category | flops | bytes accessed | tf_op | source)
XLA Modules:
  0.0 273.0 jit_solution(6957893884235910431)
XLA Ops:
  7.2 0.0 all-gather.3.cloned.1.call-start
  7.2 0.7 all-gather.3.cloned.1.call-update
  7.9 0.0 reduce-scatter.2.cloned.1.call-start
  8.0 78.3 %all-gather.3.cloned.1.call-done = bf16[2048,1024]{1,0:T(8,128)(2,1)} async-done(((bf16[256,1024]{1,0:T(8,128)(2,1)}), bf16[2048,1024]{1,0:T(8,128)(2,1)}) %all-gather.3.cloned.1.call-update) | async-done | bytes 4194320 | tf_op jit(solution)/shard_map/all_gather | solution.py:120
  86.3 2.7 constant_dynamic-slice_fusion.1
  89.0 0.0 copy-start
  89.0 1.6 copy.14
  90.6 0.1 collective-permute-start.2
  90.7 0.0 copy-done
  90.7 1.4 exponential_convert_fusion.s_ref
  92.1 1.6 copy.13
  93.7 1.1 collective-permute-done.2
  94.8 2.7 pad_maximum_fusion.1
  97.5 4.2 %copy.17 = bf16[64,8,4,1024]{3,1,2,0:T(8,128)(2,1)} copy(bf16[64,8,4,1024]{3,2,1,0:T(4,128)(2,1)S(1)} %bitcast.13) | data formatting | bytes 8388608
  101.8 24.2 %shard_map.85 = f32[512,4096]{1,0:T(8,128)} custom-call(bf16[512,4096]{1,0:T(8,128)(2,1)} %bitcast.16, bf16[4096,4096]{1,0:T(8,128)(2,1)} %c_ref.3, bf16[128,4096]{1,0:T(8,128)(2,1)} %exponential_convert_fusion.s_ref), custom_call_target="tpu_custom_call" | custom-call | flops 17179869184 | bytes 33554432 | tf_op jit(solution)/shard_map/pallas_call | solution.py:68
  126.0 0.0 copy-start.1
  126.0 0.0 copy-start.2
  126.0 2.6 slice.29
  128.6 0.2 collective-permute-start.3
  128.8 4.0 %collective-permute-done.3 = bf16[256,4096]{1,0:T(8,128)(2,1)S(1)} collective-permute-done((bf16[256,4096]{1,0:T(8,128)(2,1)S(1)}, bf16[256,4096]{1,0:T(8,128)(2,1)S(1)}, u32[]{:S(2)}, u32[]{:S(2)}) %collective-permute-start.3) | collective-permute-done | bytes 2097184 | tf_op jit(solution)/shard_map/ppermute | solution.py:142
  132.9 0.0 copy-done.1
  132.9 0.0 copy-done.2
  132.9 5.7 %multiply_convert_fusion = (bf16[256,4096]{1,0:T(8,128)(2,1)}, bf16[256,4096]{1,0:T(8,128)(2,1)}, bf16[256,4096]{1,0:T(8,128)(2,1)S(1)}) fusion(bf16[256,4096]{1,0:T(8,128)(2,1)S(1)} %collective-permute-done.3, f32[512,4096]{1,0:T(8,128)} %shard_map.85, bf16[256,4096]{1,0:T(8,128)(2,1)S(1)} %copy-done.1, bf16[256,4096]{1,0:T(8,128)(2,1)S(1)} %copy-done.2), kind=kLoop, calls=%fused_computation.18 | loop fusion | flops 19922944 | bytes 16777216 | tf_op jit(solution)/shard_map/convert_element_type | solution.py:151
  138.6 0.1 collective-permute-start
  138.7 4.0 %collective-permute-done = bf16[256,4096]{1,0:T(8,128)(2,1)S(1)} collective-permute-done((bf16[256,4096]{1,0:T(8,128)(2,1)S(1)}, bf16[256,4096]{1,0:T(8,128)(2,1)S(1)}, u32[]{:S(2)}, u32[]{:S(2)}) %collective-permute-start) | collective-permute-done | bytes 2097184 | tf_op jit(solution)/shard_map/ppermute | solution.py:126
  142.7 2.5 pad_maximum_fusion.h_ref
  145.2 23.3 %shard_map.84 = bf16[512,4096]{1,0:T(8,128)(2,1)} custom-call(bf16[512,4096]{1,0:T(8,128)(2,1)} %pad_maximum_fusion.h_ref, bf16[4096,4096]{1,0:T(8,128)(2,1)} %c_ref.3, bf16[128,4096]{1,0:T(8,128)(2,1)} %exponential_convert_fusion.s_ref), custom_call_target="tpu_custom_call" | custom-call | flops 17179869184 | bytes 33554432 | tf_op jit(solution)/shard_map/pallas_call | solution.py:36
  168.5 1.7 slice.18
  170.2 0.2 collective-permute-start.1
  170.4 4.2 %collective-permute-done.1 = bf16[256,4096]{1,0:T(8,128)(2,1)} collective-permute-done((bf16[256,4096]{1,0:T(8,128)(2,1)S(1)}, bf16[256,4096]{1,0:T(8,128)(2,1)}, u32[]{:S(2)}, u32[]{:S(2)}) %collective-permute-start.1) | collective-permute-done | bytes 2097184 | tf_op jit(solution)/shard_map/ppermute | solution.py:129
  174.6 2.5 broadcast_select_fusion.1
  177.1 0.5 copy_bitcast_fusion
  177.5 2.3 maximum_bitcast_fusion
  179.9 0.0 reduce-scatter.2.cloned.1.call-update
  179.9 23.5 %shard_map.86 = bf16[4096,4096]{1,0:T(8,128)(2,1)} custom-call(bf16[512,4096]{1,0:T(8,128)(2,1)} %pad_maximum_fusion.h_ref, bf16[512,4096]{1,0:T(8,128)(2,1)} %bitcast.17), custom_call_target="tpu_custom_call" | custom-call | flops 17179869184 | bytes 33554432 | tf_op jit(solution)/shard_map/pallas_call | solution.py:98
  203.4 62.8 %reduce-scatter.2.cloned.1.call-done = bf16[1,256,1024]{2,1,0:T(8,128)(2,1)} async-done(((bf16[8,256,1024]{2,1,0:T(8,128)(2,1)}), bf16[1,256,1024]{2,1,0:T(8,128)(2,1)}) %reduce-scatter.2.cloned.1.call-update) | async-done | bytes 524304 | tf_op jit(solution)/shard_map/reduce_scatter | solution.py:134
Async XLA Ops:
  7.2 79.1 %all-gather.3.cloned.1.call-start = ((), (), s32[]{:S(2)}) async-start(), calls=%async_computation.2 | async-start | bytes 4718592 | tf_op jit(solution)/shard_map/all_gather | solution.py:120
  7.9 258.3 %reduce-scatter.2.cloned.1.call-start = ((), (), s32[]{:S(2)}) async-start(), calls=%async_computation.1 | async-start | bytes 4718592 | tf_op jit(solution)/shard_map/reduce_scatter | solution.py:134
  89.0 1.7 copy-start
  90.6 4.2 %collective-permute-start.2 = (bf16[4,256,1024]{2,0,1:T(4,128)(2,1)S(1)}, bf16[4,256,1024]{2,0,1:T(4,128)(2,1)S(1)}, u32[]{:S(2)}, u32[]{:S(2)}) collective-permute-start(bf16[4,256,1024]{2,0,1:T(4,128)(2,1)S(1)} %copy.14), channel_id=1, source_target_pairs={{0,1},{1,0},{2,3},{3,2},{4,5},{5,4},{6,7},{7,6},{8,9},{9,8},{10,11... | collective-permute-start | bytes 6291464 | tf_op jit(solution)/shard_map/ppermute | solution.py:138
  126.0 6.9 %copy-start.1 = (bf16[256,4096]{1,0:T(8,128)(2,1)S(1)}, bf16[256,4096]{1,0:T(8,128)(2,1)}, u32[]{:S(2)}) copy-start(bf16[256,4096]{1,0:T(8,128)(2,1)} %param.5) | copy-start | bytes 6291460
  126.0 6.9 %copy-start.2 = (bf16[256,4096]{1,0:T(8,128)(2,1)S(1)}, bf16[256,4096]{1,0:T(8,128)(2,1)}, u32[]{:S(2)}) copy-start(bf16[256,4096]{1,0:T(8,128)(2,1)} %param.6) | copy-start | bytes 6291460
  128.6 4.2 %collective-permute-start.3 = (bf16[256,4096]{1,0:T(8,128)(2,1)S(1)}, bf16[256,4096]{1,0:T(8,128)(2,1)S(1)}, u32[]{:S(2)}, u32[]{:S(2)}) collective-permute-start(bf16[256,4096]{1,0:T(8,128)(2,1)S(1)} %slice.29), channel_id=1, source_target_pairs={{0,1},{1,0},{2,3},{3,2},{4,5},{5,4},{6,7},{7,6},{8,9},{9,8},{10,11... | collective-permute-start | bytes 6291464 | tf_op jit(solution)/shard_map/ppermute | solution.py:142
  138.6 4.2 %collective-permute-start = (bf16[256,4096]{1,0:T(8,128)(2,1)S(1)}, bf16[256,4096]{1,0:T(8,128)(2,1)S(1)}, u32[]{:S(2)}, u32[]{:S(2)}) collective-permute-start(bf16[256,4096]{1,0:T(8,128)(2,1)S(1)} %get-tuple-element.8), channel_id=1, source_target_pairs={{0,1},{1,0},{2,3},{3,2},{4,5},{5,4},{6,7},{7,6},{8,9},{9,8},{10,11... | collective-permute-start | bytes 6291464 | tf_op jit(solution)/shard_map/ppermute | solution.py:126
  170.2 4.4 %collective-permute-start.1 = (bf16[256,4096]{1,0:T(8,128)(2,1)S(1)}, bf16[256,4096]{1,0:T(8,128)(2,1)}, u32[]{:S(2)}, u32[]{:S(2)}) collective-permute-start(bf16[256,4096]{1,0:T(8,128)(2,1)S(1)} %slice.18), channel_id=1, source_target_pairs={{0,1},{1,0},{2,3},{3,2},{4,5},{5,4},{6,7},{7,6},{8,9},{9,8},{10,11... | collective-permute-start | bytes 6291464 | tf_op jit(solution)/shard_map/ppermute | solution.py:129
Sparse Core Ops, SparseCore 0:
  10.1 76.0 all-gather.2
  180.0 86.1 reduce-scatter.1
